TPU v7x, 256 devices: a whole 4x4x8 slice. The times are simulated.
256 devices in a mesh: table: 64 (over y, z, core), col: 4 (over x).
Axes of the slice: x: 4, y: 4, z: 8, core: 2. Of those that a mesh axis runs over, the one named last changes fastest.
Arguments:
- embedding: bfloat16 [262144, 256], P('table', 'col'), may hold values from -4 to 4
- accumulator: float32 [262144, 256], P('table', 'col'), may hold values from 0.01 to 1
- pair_rows: int32 [16384, 128, 4], P(('table', 'col')), may hold values from 0 to 1023
- pair_len: int32 [16384, 128], P(('table', 'col')), may hold values from 0 to 4
- pair_dest: int32 [256, 64], P(('table', 'col')), may hold values from 0 to 63, each once within a row
- pair_tile: int32 [256, 64], P(('table', 'col')), may hold values from 0 to 15
- pooled_grad: bfloat16 [524288, 256], P(('table', 'col')), may hold values from -6 to 6
Outputs:
- pooled: bfloat16 [524288, 256], P(('table', 'col'))
- new_embedding: bfloat16 [262144, 256], P(('table', 'col'))
- new_accumulator: float32 [262144, 256], P(('table', 'col'))
Inputs may be any that keep to these rules, and one draw needn't show every extreme that they name: `pair_dest`: each row names every table index exactly once.
All inputs are finite; a program needn't handle non-finite values.
Results may differ from a plain program's by a relative error of at most 0.0049.
Values may be sent and summed in bfloat16 or wider, within the bound.
A program may use at most 128 MiB of HBM per device.

v0:
```python
import jax
import jax.numpy as jnp
from jax import lax
from jax.sharding import PartitionSpec as P

LEARN_RATE = 0.3
EPSILON = 1e-08


def incidence(rows, lengths, width):
    valid = jnp.arange(rows.shape[-1], dtype=jnp.int32)[None, None, :] < lengths[:, :, None]
    hits = (rows[..., None] == jnp.arange(width, dtype=jnp.int32)) & valid[..., None]
    return jnp.sum(hits.astype(jnp.bfloat16), axis=2)


def move_state(accumulator):
    return lax.all_to_all(
        accumulator.astype(jnp.bfloat16), "col", split_axis=0, concat_axis=1, tiled=True
    ).astype(accumulator.dtype)


def per_device(embedding, accumulator, pair_rows, pair_len, pair_dest, pair_tile, pooled_grad):
    table_count = lax.axis_size("table")
    pair_count = pair_rows.shape[0]
    bag_rows = pair_rows.shape[1]
    width = embedding.shape[1] * lax.axis_size("col")
    tile_count = pooled_grad.shape[0] // bag_rows
    span = min(8, pair_count)
    groups = pair_count // span
    owned = lax.all_to_all(embedding, "col", split_axis=0, concat_axis=1, tiled=True)
    state = move_state(accumulator)
    row_count = owned.shape[0]
    rows_grouped = pair_rows.reshape(groups, span, bag_rows, pair_rows.shape[2])
    lens_grouped = pair_len.reshape(groups, span, bag_rows)
    dest_onehot = (
        pair_dest[0][None, :] == jnp.arange(table_count, dtype=jnp.int32)[:, None]
    ).astype(jnp.bfloat16)
    tile_marks = (pair_tile[0] + 1).astype(jnp.bfloat16)[:, None]
    send_tiles = jnp.dot(dest_onehot, tile_marks, preferred_element_type=jnp.float32).astype(
        jnp.bfloat16
    )
    tile_numbers = jnp.arange(tile_count, dtype=jnp.float32) + 1.0
    grad_tiles = pooled_grad.reshape(tile_count, bag_rows, width)

    def pool_group(item):
        rows, lengths = item
        counts = incidence(rows, lengths, row_count)
        part = jnp.einsum("gbr,rd->gbd", counts, owned, preferred_element_type=jnp.float32)
        return (part.astype(jnp.bfloat16), counts)

    partial_value, saved_counts = lax.map(pool_group, (rows_grouped, lens_grouped))
    partial_value = partial_value.reshape(pair_count, bag_rows, width)
    send_blocks = jnp.einsum(
        "np,pbd->nbd", dest_onehot, partial_value, preferred_element_type=jnp.float32
    ).astype(jnp.bfloat16)
    arrived, arrived_tiles = (
        lax.all_to_all(send_blocks, "table", split_axis=0, concat_axis=0, tiled=True),
        lax.all_to_all(send_tiles, "table", split_axis=0, concat_axis=0, tiled=True),
    )
    tile_onehot = (
        arrived_tiles[:, 0].astype(jnp.float32)[None, :] == tile_numbers[:, None]
    ).astype(jnp.bfloat16)
    back_blocks = jnp.einsum(
        "tn,tbd->nbd", tile_onehot, grad_tiles, preferred_element_type=jnp.float32
    ).astype(jnp.bfloat16)
    pooled = jnp.einsum("tn,nbd->tbd", tile_onehot, arrived, preferred_element_type=jnp.float32)
    pooled = pooled.astype(jnp.bfloat16).reshape(tile_count * bag_rows, width)
    returned = lax.all_to_all(back_blocks, "table", split_axis=0, concat_axis=0, tiled=True)
    pair_grads = jnp.einsum(
        "np,nbd->pbd", dest_onehot, returned, preferred_element_type=jnp.float32
    ).astype(jnp.bfloat16)
    pair_grads = pair_grads.reshape(groups, span, bag_rows, width)

    def add_group(total, item):
        counts, grads = item
        return (
            total + jnp.einsum("gbr,gbd->rd", counts, grads, preferred_element_type=jnp.float32),
            None,
        )

    empty = jnp.zeros((row_count, width), jnp.float32)
    grad, unused = lax.scan(add_group, empty, (saved_counts, pair_grads))
    new_state = state + grad * grad
    new_rows = (
        owned.astype(jnp.float32) - LEARN_RATE * grad / (jnp.sqrt(new_state) + EPSILON)
    ).astype(jnp.bfloat16)
    return (pooled, new_rows, new_state)


def solution(mesh):
    return jax.shard_map(
        per_device,
        mesh=mesh,
        in_specs=(
            P("table", "col"),
            P("table", "col"),
            P(("table", "col"), None, None),
            P(("table", "col"), None),
            P(("table", "col"), None),
            P(("table", "col"), None),
            P(("table", "col"), None),
        ),
        out_specs=(P(("table", "col"), None), P(("table", "col"), None), P(("table", "col"), None)),
        check_vma=False,
    )
```

profile of v0, /device:TPU:1, one launch (start us, length us, event | category | flops | bytes accessed | tf_op | source)
XLA Modules:
  0.0 259.6 jit_solution(2965978162360990122)
XLA Ops:
  2.3 13.2 %all-to-all-start = ((bf16[64,1,1]{2,1,0:T(2,128)(2,1)}), bf16[64,1,1]{2,1,0:T(2,128)(2,1)S(1)}, u32[]{:S(2)}, u32[]{:S(2)}) async-start(bf16[64,1,1]{2,1,0:T(2,128)(2,1)} %copy.86), calls=%async_computation | async-start | bytes 65536 | tf_op jit(solution)/shard_map/all_to_all | solution.py:58
  15.5 1.9 copy.137
  17.4 7.3 %all-to-all-done = bf16[64,1,1]{2,1,0:T(2,128)(2,1)S(1)} async-done(((bf16[64,1,1]{2,1,0:T(2,128)(2,1)}), bf16[64,1,1]{2,1,0:T(2,128)(2,1)S(1)}, u32[]{:S(2)}, u32[]{:S(2)}) %all-to-all-start) | async-done | bytes 160 | tf_op jit(solution)/shard_map/all_to_all | solution.py:58
  24.7 4.0 %all-to-all-start.1 = ((bf16[4,1024,64]{1,2,0:T(8,128)(2,1)}), bf16[4,1024,64]{1,2,0:T(8,128)(2,1)S(1)}, u32[]{:S(2)}, u32[]{:S(2)}) async-start(bf16[4,1024,64]{1,2,0:T(8,128)(2,1)} %bitcast.77), calls=%async_computation.1 | async-start | bytes 1048576 | tf_op jit(solution)/shard_map/all_to_all | solution.py:30
  30.8 6.2 %all-to-all-done.1 = bf16[4,1024,64]{1,2,0:T(8,128)(2,1)S(1)} async-done(((bf16[4,1024,64]{1,2,0:T(8,128)(2,1)}), bf16[4,1024,64]{1,2,0:T(8,128)(2,1)S(1)}, u32[]{:S(2)}, u32[]{:S(2)}) %all-to-all-start.1) | async-done | bytes 524320 | tf_op jit(solution)/shard_map/all_to_all | solution.py:30
  37.0 3.5 %all-to-all-start.4 = ((bf16[4,1024,64]{1,2,0:T(8,128)(2,1)}), bf16[4,1024,64]{1,2,0:T(8,128)(2,1)S(1)}, u32[]{:S(2)}, u32[]{:S(2)}) async-start(bf16[4,1024,64]{1,2,0:T(8,128)(2,1)} %bitcast.76), calls=%async_computation.4 | async-start | bytes 1048576 | tf_op jit(solution)/shard_map/all_to_all | solution.py:17
  42.4 4.4 %copy.97 = bf16[64,128,256]{2,1,0:T(8,128)(2,1)} copy(bf16[64,128,256]{2,0,1:T(8,128)(2,1)S(1)} %convolution_convert_fusion.1) | data formatting | bytes 8388608 | tf_op jit(solution)/shard_map/convert_element_type | solution.py:65
  47.5 8.4 %all-to-all-start.3 = ((bf16[64,128,256]{2,1,0:T(8,128)(2,1)}), bf16[64,128,256]{2,1,0:T(8,128)(2,1)}, u32[]{:S(2)}, u32[]{:S(2)}) async-start(bf16[64,128,256]{2,1,0:T(8,128)(2,1)} %copy.97), calls=%async_computation.3 | async-start | bytes 8388608 | tf_op jit(solution)/shard_map/all_to_all | solution.py:68
  55.9 67.5 %while.25 = (s32[]{:T(128)}, bf16[8,8,128,256]{3,2,1,0:T(8,128)(2,1)}, bf16[8,8,128,1024]{3,2,1,0:T(8,128)(2,1)}, s32[8,8,128,4]{2,3,1,0:T(4,128)}, s32[8,8,128]...) while((s32[]{:T(128)}, bf16[8,8,128,256]{3,2,1,0:T(8,128)(2,1)}, ...), condition=%wide.region_2.3_spmd, body=%wide.region_0.2_spmd.sunk | while | flops 552865792 | bytes 9572453 | solution.py:51
  57.4 4.0 %fusion.59 = bf16[8,128,1024]{2,1,0:T(8,128)(2,1)S(1)} fusion(s32[8,128,4]{1,2,0:T(4,128)S(1)} %copy.142, pred[8,128,4]{1,2,0:T(4,128)(4,1)S(1)} %iota_compare_fusion.5), kind=kLoop, calls=%fused_computation.3.clone.1 | loop fusion | flops 15728640 | bytes 2117632 | tf_op jit(solution)/shard_map/while/body/eval_jaxpr/reduce_sum | solution.py:13
  61.4 1.6 fusion.60
  62.9 1.5 bitcast_dynamic-update-slice_fusion.2
  65.9 4.0 %fusion.59 = bf16[8,128,1024]{2,1,0:T(8,128)(2,1)S(1)} fusion(s32[8,128,4]{1,2,0:T(4,128)S(1)} %copy.142, pred[8,128,4]{1,2,0:T(4,128)(4,1)S(1)} %iota_compare_fusion.5), kind=kLoop, calls=%fused_computation.3.clone.1 | loop fusion | flops 15728640 | bytes 2117632 | tf_op jit(solution)/shard_map/while/body/eval_jaxpr/reduce_sum | solution.py:13
  69.8 1.6 fusion.60
  74.3 4.0 %fusion.59 = bf16[8,128,1024]{2,1,0:T(8,128)(2,1)S(1)} fusion(s32[8,128,4]{1,2,0:T(4,128)S(1)} %copy.142, pred[8,128,4]{1,2,0:T(4,128)(4,1)S(1)} %iota_compare_fusion.5), kind=kLoop, calls=%fused_computation.3.clone.1 | loop fusion | flops 15728640 | bytes 2117632 | tf_op jit(solution)/shard_map/while/body/eval_jaxpr/reduce_sum | solution.py:13
  78.3 1.5 fusion.60
  82.7 4.0 %fusion.59 = bf16[8,128,1024]{2,1,0:T(8,128)(2,1)S(1)} fusion(s32[8,128,4]{1,2,0:T(4,128)S(1)} %copy.142, pred[8,128,4]{1,2,0:T(4,128)(4,1)S(1)} %iota_compare_fusion.5), kind=kLoop, calls=%fused_computation.3.clone.1 | loop fusion | flops 15728640 | bytes 2117632 | tf_op jit(solution)/shard_map/while/body/eval_jaxpr/reduce_sum | solution.py:13
  86.7 1.5 fusion.60
  88.2 1.5 bitcast_dynamic-update-slice_fusion.2
  91.1 4.0 %fusion.59 = bf16[8,128,1024]{2,1,0:T(8,128)(2,1)S(1)} fusion(s32[8,128,4]{1,2,0:T(4,128)S(1)} %copy.142, pred[8,128,4]{1,2,0:T(4,128)(4,1)S(1)} %iota_compare_fusion.5), kind=kLoop, calls=%fused_computation.3.clone.1 | loop fusion | flops 15728640 | bytes 2117632 | tf_op jit(solution)/shard_map/while/body/eval_jaxpr/reduce_sum | solution.py:13
  95.1 1.5 fusion.60
  96.6 1.5 bitcast_dynamic-update-slice_fusion.2
  99.6 4.0 %fusion.59 = bf16[8,128,1024]{2,1,0:T(8,128)(2,1)S(1)} fusion(s32[8,128,4]{1,2,0:T(4,128)S(1)} %copy.142, pred[8,128,4]{1,2,0:T(4,128)(4,1)S(1)} %iota_compare_fusion.5), kind=kLoop, calls=%fused_computation.3.clone.1 | loop fusion | flops 15728640 | bytes 2117632 | tf_op jit(solution)/shard_map/while/body/eval_jaxpr/reduce_sum | solution.py:13
  103.6 1.5 fusion.60
  105.1 1.5 bitcast_dynamic-update-slice_fusion.2
  108.0 4.0 %fusion.59 = bf16[8,128,1024]{2,1,0:T(8,128)(2,1)S(1)} fusion(s32[8,128,4]{1,2,0:T(4,128)S(1)} %copy.142, pred[8,128,4]{1,2,0:T(4,128)(4,1)S(1)} %iota_compare_fusion.5), kind=kLoop, calls=%fused_computation.3.clone.1 | loop fusion | flops 15728640 | bytes 2117632 | tf_op jit(solution)/shard_map/while/body/eval_jaxpr/reduce_sum | solution.py:13
  112.0 1.5 fusion.60
  116.4 4.0 %fusion.59 = bf16[8,128,1024]{2,1,0:T(8,128)(2,1)S(1)} fusion(s32[8,128,4]{1,2,0:T(4,128)S(1)} %copy.142, pred[8,128,4]{1,2,0:T(4,128)(4,1)S(1)} %iota_compare_fusion.5), kind=kLoop, calls=%fused_computation.3.clone.1 | loop fusion | flops 15728640 | bytes 2117632 | tf_op jit(solution)/shard_map/while/body/eval_jaxpr/reduce_sum | solution.py:13
  120.4 1.5 fusion.60
  123.4 5.5 %fusion.22 = bf16[64,128,256]{2,0,1:T(8,128)(2,1)S(1)} fusion(bf16[64,128,256]{2,1,0:T(8,128)(2,1)} %bitcast.98, s32[64]{0:T(128)S(1)} %bitcast.106), kind=kOutput, calls=%fused_computation.28 | convolution fusion | flops 270536704 | bytes 8388864 | tf_op jit(solution)/shard_map/np,pbd->nbd/dot_general | solution.py:53
  128.9 4.4 %copy.93 = bf16[64,128,256]{2,1,0:T(8,128)(2,1)} copy(bf16[64,128,256]{2,0,1:T(8,128)(2,1)S(1)} %fusion.22) | data formatting | bytes 8388608 | tf_op jit(solution)/shard_map/convert_element_type | solution.py:55
  133.3 18.6 %all-to-all-done.3 = bf16[64,128,256]{2,1,0:T(8,128)(2,1)} async-done(((bf16[64,128,256]{2,1,0:T(8,128)(2,1)}), bf16[64,128,256]{2,1,0:T(8,128)(2,1)}, u32[]{:S(2)}, u32[]{:S(2)}) %all-to-all-start.3) | async-done | bytes 4194336 | tf_op jit(solution)/shard_map/all_to_all | solution.py:68
  151.9 6.0 %all-to-all-start.2 = ((bf16[64,128,256]{2,1,0:T(8,128)(2,1)}), bf16[64,128,256]{2,1,0:T(8,128)(2,1)}, u32[]{:S(2)}, u32[]{:S(2)}) async-start(bf16[64,128,256]{2,1,0:T(8,128)(2,1)} %copy.93), calls=%async_computation.2 | async-start | bytes 8388608 | tf_op jit(solution)/shard_map/all_to_all | solution.py:57
  157.9 7.4 %convert_bitcast_fusion = bf16[8,8,128,256]{3,1,0,2:T(8,128)(2,1)} fusion(bf16[64,128,256]{2,1,0:T(8,128)(2,1)} %all-to-all-done.3, s32[64]{0:T(128)S(1)} %bitcast.107), kind=kOutput, calls=%fused_computation.27 | convolution fusion | flops 270536704 | bytes 8388864 | tf_op jit(solution)/shard_map/np,nbd->pbd/dot_general | solution.py:69
  165.3 37.3 %while.26 = (s32[]{:T(128)}, f32[1024,256]{1,0:T(8,128)}, bf16[8,8,128,1024]{3,2,1,0:T(8,128)(2,1)}, bf16[8,8,128,256]{3,1,0,2:T(8,128)(2,1)}, s32[]{:T(128)}, /*index=5*/s32[]{:T(128)}) while((s32[]{:T(128)}, f32[1024,256]{1,0:T(8,128)}, bf16[8,8,128,1024]{3,2,1,0:T(8,128)(2,1)}, bf16[8,8,128,256]{3,1,0,2:T(8,128)(2,1)}, ...), condition=%wide.region_4.5_spmd.clone, body=%wide.region_3.4_spmd.clone.sunk | while | flops 537395200 | bytes 5767263 | solution.py:82
  166.4 3.3 %fusion.62 = f32[1024,256]{1,0:T(8,128)} fusion(bf16[8,8,128,1024]{3,2,1,0:T(8,128)(2,1)} %get-tuple-element.309, s32[]{:T(128)S(6)} %copy.157, f32[1024,256]{1,0:T(8,128)} %get-tuple-element.302, bf16[1,8,128,256]{3,1,0,2:T(8,128)(2,1)S(1)} %constant_dynamic-slice_fusion.5, pred[]{:T(512)S(6)} %compare.3), kind=kOutput, calls=%fused_computation.17.clone.1 | convolution fusion | flops 537395200 | bytes 4718597 | tf_op jit(solution)/shard_map/while/body/eval_jaxpr/gbr,gbd->rd/dot_general | solution.py:77
  170.8 3.6 %fusion.62 = f32[1024,256]{1,0:T(8,128)} fusion(bf16[8,8,128,1024]{3,2,1,0:T(8,128)(2,1)} %get-tuple-element.309, s32[]{:T(128)S(6)} %copy.157, f32[1024,256]{1,0:T(8,128)} %get-tuple-element.302, bf16[1,8,128,256]{3,1,0,2:T(8,128)(2,1)S(1)} %constant_dynamic-slice_fusion.5, pred[]{:T(512)S(6)} %compare.3), kind=kOutput, calls=%fused_computation.17.clone.1 | convolution fusion | flops 537395200 | bytes 4718597 | tf_op jit(solution)/shard_map/while/body/eval_jaxpr/gbr,gbd->rd/dot_general | solution.py:77
  175.5 3.6 %fusion.62 = f32[1024,256]{1,0:T(8,128)} fusion(bf16[8,8,128,1024]{3,2,1,0:T(8,128)(2,1)} %get-tuple-element.309, s32[]{:T(128)S(6)} %copy.157, f32[1024,256]{1,0:T(8,128)} %get-tuple-element.302, bf16[1,8,128,256]{3,1,0,2:T(8,128)(2,1)S(1)} %constant_dynamic-slice_fusion.5, pred[]{:T(512)S(6)} %compare.3), kind=kOutput, calls=%fused_computation.17.clone.1 | convolution fusion | flops 537395200 | bytes 4718597 | tf_op jit(solution)/shard_map/while/body/eval_jaxpr/gbr,gbd->rd/dot_general | solution.py:77
  180.2 3.6 %fusion.62 = f32[1024,256]{1,0:T(8,128)} fusion(bf16[8,8,128,1024]{3,2,1,0:T(8,128)(2,1)} %get-tuple-element.309, s32[]{:T(128)S(6)} %copy.157, f32[1024,256]{1,0:T(8,128)} %get-tuple-element.302, bf16[1,8,128,256]{3,1,0,2:T(8,128)(2,1)S(1)} %constant_dynamic-slice_fusion.5, pred[]{:T(512)S(6)} %compare.3), kind=kOutput, calls=%fused_computation.17.clone.1 | convolution fusion | flops 537395200 | bytes 4718597 | tf_op jit(solution)/shard_map/while/body/eval_jaxpr/gbr,gbd->rd/dot_general | solution.py:77
  184.9 3.6 %fusion.62 = f32[1024,256]{1,0:T(8,128)} fusion(bf16[8,8,128,1024]{3,2,1,0:T(8,128)(2,1)} %get-tuple-element.309, s32[]{:T(128)S(6)} %copy.157, f32[1024,256]{1,0:T(8,128)} %get-tuple-element.302, bf16[1,8,128,256]{3,1,0,2:T(8,128)(2,1)S(1)} %constant_dynamic-slice_fusion.5, pred[]{:T(512)S(6)} %compare.3), kind=kOutput, calls=%fused_computation.17.clone.1 | convolution fusion | flops 537395200 | bytes 4718597 | tf_op jit(solution)/shard_map/while/body/eval_jaxpr/gbr,gbd->rd/dot_general | solution.py:77
  189.6 3.6 %fusion.62 = f32[1024,256]{1,0:T(8,128)} fusion(bf16[8,8,128,1024]{3,2,1,0:T(8,128)(2,1)} %get-tuple-element.309, s32[]{:T(128)S(6)} %copy.157, f32[1024,256]{1,0:T(8,128)} %get-tuple-element.302, bf16[1,8,128,256]{3,1,0,2:T(8,128)(2,1)S(1)} %constant_dynamic-slice_fusion.5, pred[]{:T(512)S(6)} %compare.3), kind=kOutput, calls=%fused_computation.17.clone.1 | convolution fusion | flops 537395200 | bytes 4718597 | tf_op jit(solution)/shard_map/while/body/eval_jaxpr/gbr,gbd->rd/dot_general | solution.py:77
  194.2 3.6 %fusion.62 = f32[1024,256]{1,0:T(8,128)} fusion(bf16[8,8,128,1024]{3,2,1,0:T(8,128)(2,1)} %get-tuple-element.309, s32[]{:T(128)S(6)} %copy.157, f32[1024,256]{1,0:T(8,128)} %get-tuple-element.302, bf16[1,8,128,256]{3,1,0,2:T(8,128)(2,1)S(1)} %constant_dynamic-slice_fusion.5, pred[]{:T(512)S(6)} %compare.3), kind=kOutput, calls=%fused_computation.17.clone.1 | convolution fusion | flops 537395200 | bytes 4718597 | tf_op jit(solution)/shard_map/while/body/eval_jaxpr/gbr,gbd->rd/dot_general | solution.py:77
  198.9 3.6 %fusion.62 = f32[1024,256]{1,0:T(8,128)} fusion(bf16[8,8,128,1024]{3,2,1,0:T(8,128)(2,1)} %get-tuple-element.309, s32[]{:T(128)S(6)} %copy.157, f32[1024,256]{1,0:T(8,128)} %get-tuple-element.302, bf16[1,8,128,256]{3,1,0,2:T(8,128)(2,1)S(1)} %constant_dynamic-slice_fusion.5, pred[]{:T(512)S(6)} %compare.3), kind=kOutput, calls=%fused_computation.17.clone.1 | convolution fusion | flops 537395200 | bytes 4718597 | tf_op jit(solution)/shard_map/while/body/eval_jaxpr/gbr,gbd->rd/dot_general | solution.py:77
  202.5 2.5 copy.101
  205.1 2.6 bitcast_add_fusion
  207.7 2.0 copy.105
  211.0 42.7 %all-to-all-done.2 = bf16[64,128,256]{2,1,0:T(8,128)(2,1)} async-done(((bf16[64,128,256]{2,1,0:T(8,128)(2,1)}), bf16[64,128,256]{2,1,0:T(8,128)(2,1)}, u32[]{:S(2)}, u32[]{:S(2)}) %all-to-all-start.2) | async-done | bytes 4194336 | tf_op jit(solution)/shard_map/all_to_all | solution.py:57
  253.7 4.5 %fusion.27 = bf16[16,128,256]{2,0,1:T(8,128)(2,1)S(1)} fusion(bf16[64,128,256]{2,1,0:T(8,128)(2,1)} %all-to-all-done.2, f32[64]{0:T(128)S(1)} %convert_reduce_fusion, f32[16]{0:T(128)S(1)} %iota_add_fusion), kind=kOutput, calls=%fused_computation.30 | convolution fusion | flops 67634176 | bytes 5243200 | tf_op jit(solution)/shard_map/tn,nbd->tbd/dot_general | solution.py:66
  (70 shorter events, 35.1 us)
Async XLA Ops:
  0.6 40.4 %copy-start = (bf16[2048,256]{1,0:T(8,128)(2,1)S(1)}, bf16[2048,256]{1,0:T(8,128)(2,1)}, u32[]{:S(2)}) copy-start(bf16[2048,256]{1,0:T(8,128)(2,1)} %param.17) | copy-start | bytes 3145732
  2.3 22.4 %all-to-all-start = ((bf16[64,1,1]{2,1,0:T(2,128)(2,1)}), bf16[64,1,1]{2,1,0:T(2,128)(2,1)S(1)}, u32[]{:S(2)}, u32[]{:S(2)}) async-start(bf16[64,1,1]{2,1,0:T(2,128)(2,1)} %copy.86), calls=%async_computation | async-start | bytes 65536 | tf_op jit(solution)/shard_map/all_to_all | solution.py:58
  24.7 12.3 %all-to-all-start.1 = ((bf16[4,1024,64]{1,2,0:T(8,128)(2,1)}), bf16[4,1024,64]{1,2,0:T(8,128)(2,1)S(1)}, u32[]{:S(2)}, u32[]{:S(2)}) async-start(bf16[4,1024,64]{1,2,0:T(8,128)(2,1)} %bitcast.77), calls=%async_computation.1 | async-start | bytes 1048576 | tf_op jit(solution)/shard_map/all_to_all | solution.py:30
  37.0 10.5 %all-to-all-start.4 = ((bf16[4,1024,64]{1,2,0:T(8,128)(2,1)}), bf16[4,1024,64]{1,2,0:T(8,128)(2,1)S(1)}, u32[]{:S(2)}, u32[]{:S(2)}) async-start(bf16[4,1024,64]{1,2,0:T(8,128)(2,1)} %bitcast.76), calls=%async_computation.4 | async-start | bytes 1048576 | tf_op jit(solution)/shard_map/all_to_all | solution.py:17
  47.5 104.3 %all-to-all-start.3 = ((bf16[64,128,256]{2,1,0:T(8,128)(2,1)}), bf16[64,128,256]{2,1,0:T(8,128)(2,1)}, u32[]{:S(2)}, u32[]{:S(2)}) async-start(bf16[64,128,256]{2,1,0:T(8,128)(2,1)} %copy.97), calls=%async_computation.3 | async-start | bytes 8388608 | tf_op jit(solution)/shard_map/all_to_all | solution.py:68
  55.9 67.5 %copy-start.1 = (s32[1,64]{1,0:T(1,128)S(1)}, s32[1,64]{1,0:T(1,128)}, u32[]{:S(2)}) copy-start(s32[1,64]{1,0:T(1,128)} %param.15) | copy-start | bytes 772
  151.9 101.9 %all-to-all-start.2 = ((bf16[64,128,256]{2,1,0:T(8,128)(2,1)}), bf16[64,128,256]{2,1,0:T(8,128)(2,1)}, u32[]{:S(2)}, u32[]{:S(2)}) async-start(bf16[64,128,256]{2,1,0:T(8,128)(2,1)} %copy.93), calls=%async_computation.2 | async-start | bytes 8388608 | tf_op jit(solution)/shard_map/all_to_all | solution.py:57
where the time goes:
time: 261 us; the launch traced here: 260 us
  waiting for transfers between devices  75.3 us (29%)
  matrix products  60.5 us (23%)
  local copies, waits for them, and re-layouts  51.6 us (20%)
  other arithmetic  36.2 us (14%)
  starting transfers between devices  35.1 us (13%)
    all_to_all x1, waiting for transfers between devices, per_device(): lax.all_to_all(send_blocks, 'table', split_axis=0, concat_axis=0, tiled=T...  42.7 us
    reduce_sum x8, other arithmetic, incidence(): return jnp.sum(hits.astype(jnp.bfloat16), axis=2)  31.6 us
    dot_general x8, matrix products, add_group(): jnp.einsum('gbr,gbd->rd', counts, grads, preferred_element_type=jnp.float32)  28.6 us
    all_to_all x1, waiting for transfers between devices, per_device(): lax.all_to_all(back_blocks, 'table', split_axis=0, concat_axis=0, tiled=T...  18.6 us
    all_to_all x1, starting transfers between devices, per_device(): lax.all_to_all(send_tiles, 'table', split_axis=0, concat_axis=0, tiled=True)  13.2 us
    dot_general x8, matrix products, pool_group(): jnp.einsum('gbr,rd->gbd', counts, owned, preferred_element_type=jnp.float32)  12.2 us
    dynamic_update_slice x8, local copies, waits for them, and re-layouts, per_device(): lax.map(pool_group, (rows_grouped, lens_grouped))  12 us
    dynamic_slice x8, local copies, waits for them, and re-layouts, per_device(): grad, unused = lax.scan(add_group, empty, (saved_counts, pair_grads))  8.6 us
  transfers between devices with their start and end apart: 5, of which 5 were waited for; matrix products, arithmetic and copies ran while one was open for 54% of the time, Pallas kernels for 0%

commit v1 on v0

--- a/solution.py
+++ b/solution.py
@@ -27,7 +27,9 @@
     tile_count = pooled_grad.shape[0] // bag_rows
     span = min(8, pair_count)
     groups = pair_count // span
-    owned = lax.all_to_all(embedding, "col", split_axis=0, concat_axis=1, tiled=True)
+    cells = jnp.split(embedding, lax.axis_size("col"), axis=0)
+    received = lax.all_to_all(jnp.stack(cells), "col", 0, 0)
+    owned = jnp.concatenate(received, axis=1)
     state = move_state(accumulator)
     row_count = owned.shape[0]
     rows_grouped = pair_rows.reshape(groups, span, bag_rows, pair_rows.shape[2])

time: 261 us -> 261 us (level)
  no operation moved by 1% of the time
where the time goes in v1:
time: 261 us; the launch traced here: 260 us
  waiting for transfers between devices  75.8 us (29%)
  matrix products  60.6 us (23%)
  local copies, waits for them, and re-layouts  51.1 us (20%)
  other arithmetic  36.2 us (14%)
  starting transfers between devices  35.1 us (13%)
    all_to_all x1, waiting for transfers between devices, per_device(): lax.all_to_all(send_blocks, 'table', split_axis=0, concat_axis=0, tiled=T...  43.3 us
    reduce_sum x8, other arithmetic, incidence(): return jnp.sum(hits.astype(jnp.bfloat16), axis=2)  31.6 us
    dot_general x8, matrix products, add_group(): jnp.einsum('gbr,gbd->rd', counts, grads, preferred_element_type=jnp.float32)  28.6 us
    all_to_all x1, waiting for transfers between devices, per_device(): lax.all_to_all(back_blocks, 'table', split_axis=0, concat_axis=0, tiled=T...  18.5 us
    all_to_all x1, starting transfers between devices, per_device(): lax.all_to_all(send_tiles, 'table', split_axis=0, concat_axis=0, tiled=True)  13.2 us
    dot_general x8, matrix products, pool_group(): jnp.einsum('gbr,rd->gbd', counts, owned, preferred_element_type=jnp.float32)  12.3 us
    dynamic_update_slice x8, local copies, waits for them, and re-layouts, per_device(): lax.map(pool_group, (rows_grouped, lens_grouped))  12 us
    dynamic_slice x8, local copies, waits for them, and re-layouts, per_device(): grad, unused = lax.scan(add_group, empty, (saved_counts, pair_grads))  8.6 us
  transfers between devices with their start and end apart: 5, of which 5 were waited for; matrix products, arithmetic and copies ran while one was open for 54% of the time, Pallas kernels for 0%

profile of v1, /device:TPU:1, one launch (start us, length us, event | category | flops | bytes accessed | tf_op | source)
XLA Modules:
  0.0 259.6 jit_solution(669951487323519894)
XLA Ops:
  2.3 13.2 %all-to-all-start = ((bf16[64,1,1]{2,1,0:T(2,128)(2,1)}), bf16[64,1,1]{2,1,0:T(2,128)(2,1)S(1)}, u32[]{:S(2)}, u32[]{:S(2)}) async-start(bf16[64,1,1]{2,1,0:T(2,128)(2,1)} %copy.83), calls=%async_computation | async-start | bytes 65536 | tf_op jit(solution)/shard_map/all_to_all | solution.py:60
  17.5 7.2 %all-to-all-done = bf16[64,1,1]{2,1,0:T(2,128)(2,1)S(1)} async-done(((bf16[64,1,1]{2,1,0:T(2,128)(2,1)}), bf16[64,1,1]{2,1,0:T(2,128)(2,1)S(1)}, u32[]{:S(2)}, u32[]{:S(2)}) %all-to-all-start) | async-done | bytes 160 | tf_op jit(solution)/shard_map/all_to_all | solution.py:60
  24.7 4.0 %all-to-all-start.1 = ((bf16[4,1024,64]{1,2,0:T(8,128)(2,1)}), bf16[4,1024,64]{1,2,0:T(8,128)(2,1)S(1)}, u32[]{:S(2)}, u32[]{:S(2)}) async-start(bf16[4,1024,64]{1,2,0:T(8,128)(2,1)} %pad_maximum_fusion), calls=%async_computation.1 | async-start | bytes 1048576 | tf_op jit(solution)/shard_map/all_to_all | solution.py:31
  30.9 6.2 %all-to-all-done.1 = bf16[4,1024,64]{1,2,0:T(8,128)(2,1)S(1)} async-done(((bf16[4,1024,64]{1,2,0:T(8,128)(2,1)}), bf16[4,1024,64]{1,2,0:T(8,128)(2,1)S(1)}, u32[]{:S(2)}, u32[]{:S(2)}) %all-to-all-start.1) | async-done | bytes 524320 | tf_op jit(solution)/shard_map/all_to_all | solution.py:31
  37.0 3.5 %all-to-all-start.4 = ((bf16[4,1024,64]{1,2,0:T(8,128)(2,1)}), bf16[4,1024,64]{1,2,0:T(8,128)(2,1)S(1)}, u32[]{:S(2)}, u32[]{:S(2)}) async-start(bf16[4,1024,64]{1,2,0:T(8,128)(2,1)} %bitcast.81), calls=%async_computation.4 | async-start | bytes 1048576 | tf_op jit(solution)/shard_map/all_to_all | solution.py:17
  42.4 4.4 %copy.93 = bf16[64,128,256]{2,1,0:T(8,128)(2,1)} copy(bf16[64,128,256]{2,0,1:T(8,128)(2,1)S(1)} %convolution_convert_fusion.1) | data formatting | bytes 8388608 | tf_op jit(solution)/shard_map/convert_element_type | solution.py:67
  47.5 8.4 %all-to-all-start.3 = ((bf16[64,128,256]{2,1,0:T(8,128)(2,1)}), bf16[64,128,256]{2,1,0:T(8,128)(2,1)}, u32[]{:S(2)}, u32[]{:S(2)}) async-start(bf16[64,128,256]{2,1,0:T(8,128)(2,1)} %copy.93), calls=%async_computation.3 | async-start | bytes 8388608 | tf_op jit(solution)/shard_map/all_to_all | solution.py:70
  55.9 67.5 %while.25 = (s32[]{:T(128)}, bf16[8,8,128,256]{3,2,1,0:T(8,128)(2,1)}, bf16[8,8,128,1024]{3,2,1,0:T(8,128)(2,1)}, s32[8,8,128,4]{2,3,1,0:T(4,128)}, s32[8,8,128]...) while((s32[]{:T(128)}, bf16[8,8,128,256]{3,2,1,0:T(8,128)(2,1)}, ...), condition=%wide.region_2.3_spmd, body=%wide.region_0.2_spmd.sunk | while | flops 552865792 | bytes 9573461 | solution.py:53
  57.4 4.0 %fusion.59 = bf16[8,128,1024]{2,1,0:T(8,128)(2,1)S(1)} fusion(s32[8,128,4]{1,2,0:T(4,128)S(1)} %copy.135, pred[8,128,4]{1,2,0:T(4,128)(4,1)S(1)} %iota_compare_fusion.5), kind=kLoop, calls=%fused_computation.3.clone.1 | loop fusion | flops 15728640 | bytes 2117632 | tf_op jit(solution)/shard_map/while/body/eval_jaxpr/reduce_sum | solution.py:13
  61.4 1.6 fusion.60
  62.9 1.5 bitcast_dynamic-update-slice_fusion.2
  65.8 4.0 %fusion.59 = bf16[8,128,1024]{2,1,0:T(8,128)(2,1)S(1)} fusion(s32[8,128,4]{1,2,0:T(4,128)S(1)} %copy.135, pred[8,128,4]{1,2,0:T(4,128)(4,1)S(1)} %iota_compare_fusion.5), kind=kLoop, calls=%fused_computation.3.clone.1 | loop fusion | flops 15728640 | bytes 2117632 | tf_op jit(solution)/shard_map/while/body/eval_jaxpr/reduce_sum | solution.py:13
  69.8 1.6 fusion.60
  74.3 4.0 %fusion.59 = bf16[8,128,1024]{2,1,0:T(8,128)(2,1)S(1)} fusion(s32[8,128,4]{1,2,0:T(4,128)S(1)} %copy.135, pred[8,128,4]{1,2,0:T(4,128)(4,1)S(1)} %iota_compare_fusion.5), kind=kLoop, calls=%fused_computation.3.clone.1 | loop fusion | flops 15728640 | bytes 2117632 | tf_op jit(solution)/shard_map/while/body/eval_jaxpr/reduce_sum | solution.py:13
  78.3 1.5 fusion.60
  82.7 4.0 %fusion.59 = bf16[8,128,1024]{2,1,0:T(8,128)(2,1)S(1)} fusion(s32[8,128,4]{1,2,0:T(4,128)S(1)} %copy.135, pred[8,128,4]{1,2,0:T(4,128)(4,1)S(1)} %iota_compare_fusion.5), kind=kLoop, calls=%fused_computation.3.clone.1 | loop fusion | flops 15728640 | bytes 2117632 | tf_op jit(solution)/shard_map/while/body/eval_jaxpr/reduce_sum | solution.py:13
  86.7 1.5 fusion.60
  88.2 1.5 bitcast_dynamic-update-slice_fusion.2
  91.2 4.0 %fusion.59 = bf16[8,128,1024]{2,1,0:T(8,128)(2,1)S(1)} fusion(s32[8,128,4]{1,2,0:T(4,128)S(1)} %copy.135, pred[8,128,4]{1,2,0:T(4,128)(4,1)S(1)} %iota_compare_fusion.5), kind=kLoop, calls=%fused_computation.3.clone.1 | loop fusion | flops 15728640 | bytes 2117632 | tf_op jit(solution)/shard_map/while/body/eval_jaxpr/reduce_sum | solution.py:13
  95.1 1.5 fusion.60
  96.7 1.5 bitcast_dynamic-update-slice_fusion.2
  99.6 4.0 %fusion.59 = bf16[8,128,1024]{2,1,0:T(8,128)(2,1)S(1)} fusion(s32[8,128,4]{1,2,0:T(4,128)S(1)} %copy.135, pred[8,128,4]{1,2,0:T(4,128)(4,1)S(1)} %iota_compare_fusion.5), kind=kLoop, calls=%fused_computation.3.clone.1 | loop fusion | flops 15728640 | bytes 2117632 | tf_op jit(solution)/shard_map/while/body/eval_jaxpr/reduce_sum | solution.py:13
  103.6 1.5 fusion.60
  105.1 1.5 bitcast_dynamic-update-slice_fusion.2
  108.1 4.0 %fusion.59 = bf16[8,128,1024]{2,1,0:T(8,128)(2,1)S(1)} fusion(s32[8,128,4]{1,2,0:T(4,128)S(1)} %copy.135, pred[8,128,4]{1,2,0:T(4,128)(4,1)S(1)} %iota_compare_fusion.5), kind=kLoop, calls=%fused_computation.3.clone.1 | loop fusion | flops 15728640 | bytes 2117632 | tf_op jit(solution)/shard_map/while/body/eval_jaxpr/reduce_sum | solution.py:13
  112.0 1.5 fusion.60
  116.5 4.0 %fusion.59 = bf16[8,128,1024]{2,1,0:T(8,128)(2,1)S(1)} fusion(s32[8,128,4]{1,2,0:T(4,128)S(1)} %copy.135, pred[8,128,4]{1,2,0:T(4,128)(4,1)S(1)} %iota_compare_fusion.5), kind=kLoop, calls=%fused_computation.3.clone.1 | loop fusion | flops 15728640 | bytes 2117632 | tf_op jit(solution)/shard_map/while/body/eval_jaxpr/reduce_sum | solution.py:13
  120.4 1.5 fusion.60
  123.4 5.5 %fusion.22 = bf16[64,128,256]{2,0,1:T(8,128)(2,1)S(1)} fusion(bf16[64,128,256]{2,1,0:T(8,128)(2,1)} %bitcast.102, s32[64]{0:T(128)S(1)} %bitcast.109), kind=kOutput, calls=%fused_computation.28 | convolution fusion | flops 270536704 | bytes 8388864 | tf_op jit(solution)/shard_map/np,pbd->nbd/dot_general | solution.py:55
  128.9 4.4 %copy.89 = bf16[64,128,256]{2,1,0:T(8,128)(2,1)} copy(bf16[64,128,256]{2,0,1:T(8,128)(2,1)S(1)} %fusion.22) | data formatting | bytes 8388608 | tf_op jit(solution)/shard_map/convert_element_type | solution.py:57
  133.3 18.5 %all-to-all-done.3 = bf16[64,128,256]{2,1,0:T(8,128)(2,1)} async-done(((bf16[64,128,256]{2,1,0:T(8,128)(2,1)}), bf16[64,128,256]{2,1,0:T(8,128)(2,1)}, u32[]{:S(2)}, u32[]{:S(2)}) %all-to-all-start.3) | async-done | bytes 4194336 | tf_op jit(solution)/shard_map/all_to_all | solution.py:70
  151.8 6.0 %all-to-all-start.2 = ((bf16[64,128,256]{2,1,0:T(8,128)(2,1)}), bf16[64,128,256]{2,1,0:T(8,128)(2,1)}, u32[]{:S(2)}, u32[]{:S(2)}) async-start(bf16[64,128,256]{2,1,0:T(8,128)(2,1)} %copy.89), calls=%async_computation.2 | async-start | bytes 8388608 | tf_op jit(solution)/shard_map/all_to_all | solution.py:59
  157.9 7.4 %convert_bitcast_fusion = bf16[8,8,128,256]{3,1,0,2:T(8,128)(2,1)} fusion(bf16[64,128,256]{2,1,0:T(8,128)(2,1)} %all-to-all-done.3, s32[64]{0:T(128)S(1)} %bitcast.110), kind=kOutput, calls=%fused_computation.27 | convolution fusion | flops 270536704 | bytes 8388864 | tf_op jit(solution)/shard_map/np,nbd->pbd/dot_general | solution.py:71
  165.3 37.3 %while.26 = (s32[]{:T(128)}, f32[1024,256]{1,0:T(8,128)}, bf16[8,8,128,1024]{3,2,1,0:T(8,128)(2,1)}, bf16[8,8,128,256]{3,1,0,2:T(8,128)(2,1)}, s32[]{:T(128)}, /*index=5*/s32[]{:T(128)}) while((s32[]{:T(128)}, f32[1024,256]{1,0:T(8,128)}, bf16[8,8,128,1024]{3,2,1,0:T(8,128)(2,1)}, bf16[8,8,128,256]{3,1,0,2:T(8,128)(2,1)}, ...), condition=%wide.region_4.5_spmd.clone, body=%wide.region_3.4_spmd.clone.sunk | while | flops 537395200 | bytes 5767763 | solution.py:84
  166.4 3.3 %fusion.62 = f32[1024,256]{1,0:T(8,128)} fusion(bf16[8,8,128,1024]{3,2,1,0:T(8,128)(2,1)} %get-tuple-element.313, s32[]{:T(128)} %get-tuple-element.305, f32[1024,256]{1,0:T(8,128)} %get-tuple-element.306, bf16[1,8,128,256]{3,1,0,2:T(8,128)(2,1)S(1)} %constant_dynamic-slice_fusion.5, pred[]{:T(512)S(6)} %compare.3), kind=kOutput, calls=%fused_computation.17.clone.1 | convolution fusion | flops 537395200 | bytes 4719105 | tf_op jit(solution)/shard_map/while/body/eval_jaxpr/gbr,gbd->rd/dot_general | solution.py:79
  170.8 3.6 %fusion.62 = f32[1024,256]{1,0:T(8,128)} fusion(bf16[8,8,128,1024]{3,2,1,0:T(8,128)(2,1)} %get-tuple-element.313, s32[]{:T(128)} %get-tuple-element.305, f32[1024,256]{1,0:T(8,128)} %get-tuple-element.306, bf16[1,8,128,256]{3,1,0,2:T(8,128)(2,1)S(1)} %constant_dynamic-slice_fusion.5, pred[]{:T(512)S(6)} %compare.3), kind=kOutput, calls=%fused_computation.17.clone.1 | convolution fusion | flops 537395200 | bytes 4719105 | tf_op jit(solution)/shard_map/while/body/eval_jaxpr/gbr,gbd->rd/dot_general | solution.py:79
  175.5 3.6 %fusion.62 = f32[1024,256]{1,0:T(8,128)} fusion(bf16[8,8,128,1024]{3,2,1,0:T(8,128)(2,1)} %get-tuple-element.313, s32[]{:T(128)} %get-tuple-element.305, f32[1024,256]{1,0:T(8,128)} %get-tuple-element.306, bf16[1,8,128,256]{3,1,0,2:T(8,128)(2,1)S(1)} %constant_dynamic-slice_fusion.5, pred[]{:T(512)S(6)} %compare.3), kind=kOutput, calls=%fused_computation.17.clone.1 | convolution fusion | flops 537395200 | bytes 4719105 | tf_op jit(solution)/shard_map/while/body/eval_jaxpr/gbr,gbd->rd/dot_general | solution.py:79
  180.2 3.6 %fusion.62 = f32[1024,256]{1,0:T(8,128)} fusion(bf16[8,8,128,1024]{3,2,1,0:T(8,128)(2,1)} %get-tuple-element.313, s32[]{:T(128)} %get-tuple-element.305, f32[1024,256]{1,0:T(8,128)} %get-tuple-element.306, bf16[1,8,128,256]{3,1,0,2:T(8,128)(2,1)S(1)} %constant_dynamic-slice_fusion.5, pred[]{:T(512)S(6)} %compare.3), kind=kOutput, calls=%fused_computation.17.clone.1 | convolution fusion | flops 537395200 | bytes 4719105 | tf_op jit(solution)/shard_map/while/body/eval_jaxpr/gbr,gbd->rd/dot_general | solution.py:79
  184.9 3.6 %fusion.62 = f32[1024,256]{1,0:T(8,128)} fusion(bf16[8,8,128,1024]{3,2,1,0:T(8,128)(2,1)} %get-tuple-element.313, s32[]{:T(128)} %get-tuple-element.305, f32[1024,256]{1,0:T(8,128)} %get-tuple-element.306, bf16[1,8,128,256]{3,1,0,2:T(8,128)(2,1)S(1)} %constant_dynamic-slice_fusion.5, pred[]{:T(512)S(6)} %compare.3), kind=kOutput, calls=%fused_computation.17.clone.1 | convolution fusion | flops 537395200 | bytes 4719105 | tf_op jit(solution)/shard_map/while/body/eval_jaxpr/gbr,gbd->rd/dot_general | solution.py:79
  189.6 3.6 %fusion.62 = f32[1024,256]{1,0:T(8,128)} fusion(bf16[8,8,128,1024]{3,2,1,0:T(8,128)(2,1)} %get-tuple-element.313, s32[]{:T(128)} %get-tuple-element.305, f32[1024,256]{1,0:T(8,128)} %get-tuple-element.306, bf16[1,8,128,256]{3,1,0,2:T(8,128)(2,1)S(1)} %constant_dynamic-slice_fusion.5, pred[]{:T(512)S(6)} %compare.3), kind=kOutput, calls=%fused_computation.17.clone.1 | convolution fusion | flops 537395200 | bytes 4719105 | tf_op jit(solution)/shard_map/while/body/eval_jaxpr/gbr,gbd->rd/dot_general | solution.py:79
  194.2 3.6 %fusion.62 = f32[1024,256]{1,0:T(8,128)} fusion(bf16[8,8,128,1024]{3,2,1,0:T(8,128)(2,1)} %get-tuple-element.313, s32[]{:T(128)} %get-tuple-element.305, f32[1024,256]{1,0:T(8,128)} %get-tuple-element.306, bf16[1,8,128,256]{3,1,0,2:T(8,128)(2,1)S(1)} %constant_dynamic-slice_fusion.5, pred[]{:T(512)S(6)} %compare.3), kind=kOutput, calls=%fused_computation.17.clone.1 | convolution fusion | flops 537395200 | bytes 4719105 | tf_op jit(solution)/shard_map/while/body/eval_jaxpr/gbr,gbd->rd/dot_general | solution.py:79
  198.9 3.6 %fusion.62 = f32[1024,256]{1,0:T(8,128)} fusion(bf16[8,8,128,1024]{3,2,1,0:T(8,128)(2,1)} %get-tuple-element.313, s32[]{:T(128)} %get-tuple-element.305, f32[1024,256]{1,0:T(8,128)} %get-tuple-element.306, bf16[1,8,128,256]{3,1,0,2:T(8,128)(2,1)S(1)} %constant_dynamic-slice_fusion.5, pred[]{:T(512)S(6)} %compare.3), kind=kOutput, calls=%fused_computation.17.clone.1 | convolution fusion | flops 537395200 | bytes 4719105 | tf_op jit(solution)/shard_map/while/body/eval_jaxpr/gbr,gbd->rd/dot_general | solution.py:79
  202.5 1.6 copy.97
  204.1 1.7 bitcast_add_fusion
  205.8 2.5 copy.102
  208.4 2.0 copy.101
  210.4 43.3 %all-to-all-done.2 = bf16[64,128,256]{2,1,0:T(8,128)(2,1)} async-done(((bf16[64,128,256]{2,1,0:T(8,128)(2,1)}), bf16[64,128,256]{2,1,0:T(8,128)(2,1)}, u32[]{:S(2)}, u32[]{:S(2)}) %all-to-all-start.2) | async-done | bytes 4194336 | tf_op jit(solution)/shard_map/all_to_all | solution.py:59
  253.7 4.5 %fusion.27 = bf16[16,128,256]{2,0,1:T(8,128)(2,1)S(1)} fusion(bf16[64,128,256]{2,1,0:T(8,128)(2,1)} %all-to-all-done.2, f32[64]{0:T(128)S(1)} %convert_reduce_fusion, f32[16]{0:T(128)S(1)} %iota_add_fusion), kind=kOutput, calls=%fused_computation.30 | convolution fusion | flops 67634176 | bytes 5243200 | tf_op jit(solution)/shard_map/tn,nbd->tbd/dot_general | solution.py:68
  (71 shorter events, 35.8 us)
Async XLA Ops:
  0.6 40.4 %copy-start = (bf16[2048,256]{1,0:T(8,128)(2,1)S(1)}, bf16[2048,256]{1,0:T(8,128)(2,1)}, u32[]{:S(2)}) copy-start(bf16[2048,256]{1,0:T(8,128)(2,1)} %param.17) | copy-start | bytes 3145732
  2.3 22.4 %all-to-all-start = ((bf16[64,1,1]{2,1,0:T(2,128)(2,1)}), bf16[64,1,1]{2,1,0:T(2,128)(2,1)S(1)}, u32[]{:S(2)}, u32[]{:S(2)}) async-start(bf16[64,1,1]{2,1,0:T(2,128)(2,1)} %copy.83), calls=%async_computation | async-start | bytes 65536 | tf_op jit(solution)/shard_map/all_to_all | solution.py:60
  24.7 12.3 %all-to-all-start.1 = ((bf16[4,1024,64]{1,2,0:T(8,128)(2,1)}), bf16[4,1024,64]{1,2,0:T(8,128)(2,1)S(1)}, u32[]{:S(2)}, u32[]{:S(2)}) async-start(bf16[4,1024,64]{1,2,0:T(8,128)(2,1)} %pad_maximum_fusion), calls=%async_computation.1 | async-start | bytes 1048576 | tf_op jit(solution)/shard_map/all_to_all | solution.py:31
  37.0 10.5 %all-to-all-start.4 = ((bf16[4,1024,64]{1,2,0:T(8,128)(2,1)}), bf16[4,1024,64]{1,2,0:T(8,128)(2,1)S(1)}, u32[]{:S(2)}, u32[]{:S(2)}) async-start(bf16[4,1024,64]{1,2,0:T(8,128)(2,1)} %bitcast.81), calls=%async_computation.4 | async-start | bytes 1048576 | tf_op jit(solution)/shard_map/all_to_all | solution.py:17
  47.5 104.3 %all-to-all-start.3 = ((bf16[64,128,256]{2,1,0:T(8,128)(2,1)}), bf16[64,128,256]{2,1,0:T(8,128)(2,1)}, u32[]{:S(2)}, u32[]{:S(2)}) async-start(bf16[64,128,256]{2,1,0:T(8,128)(2,1)} %copy.93), calls=%async_computation.3 | async-start | bytes 8388608 | tf_op jit(solution)/shard_map/all_to_all | solution.py:70
  55.9 67.5 %copy-start.1 = (s32[1,64]{1,0:T(1,128)S(1)}, s32[1,64]{1,0:T(1,128)}, u32[]{:S(2)}) copy-start(s32[1,64]{1,0:T(1,128)} %param.15) | copy-start | bytes 772
  151.8 101.9 %all-to-all-start.2 = ((bf16[64,128,256]{2,1,0:T(8,128)(2,1)}), bf16[64,128,256]{2,1,0:T(8,128)(2,1)}, u32[]{:S(2)}, u32[]{:S(2)}) async-start(bf16[64,128,256]{2,1,0:T(8,128)(2,1)} %copy.89), calls=%async_computation.2 | async-start | bytes 8388608 | tf_op jit(solution)/shard_map/all_to_all | solution.py:59
